TPU v7x, 256 devices: a whole 4x4x8 slice. The times are simulated.
256 devices in a mesh: row: 16 (over x, y_hi, core), col: 16 (over y_lo, z).
Axes of the slice: x: 4, y: 4 (y_hi: 2, y_lo: 2; y = y_hi * 2 + y_lo), z: 8, core: 2. Of those that a mesh axis runs over, the one named last changes fastest.
Arguments:
- x_matrix: float32 [16384, 16384], P('row', 'col'), as said below
- h_matrix: float32 [16384, 16384], P('row', 'col'), as said below
- x_mask: int32 [128, 128], P('row', 'col'), may hold values from 0 to 1, as said below
- h_mask: int32 [128, 128], P('row', 'col'), may hold values from 0 to 1, as said below
- panel: int32 [1], replicated, may hold values from 0 to 31
Outputs:
- congruence: float32 [512, 16384], P('row', 'col')
Inputs may be any that keep to these rules, and one draw needn't show every extreme that they name: x_matrix is symmetric. h_matrix is symmetric. `x_mask`: symmetric 0/1 pattern with ones on the diagonal; most occupied blocks lie near the diagonal, with wrap around, or near the wrapped block distance 128 // 4, and a few other blocks are scattered. `h_mask`: symmetric 0/1 pattern with ones on the diagonal; most occupied blocks lie near the diagonal, with wrap around, or near the wrapped block distance 128 // 4, and a few other blocks are scattered.
All inputs are finite; a program needn't handle non-finite values.
Results may differ from a plain program's by a relative error of at most 0.000094.
Values sent between devices are 32-bit elements; how exact they have to be, the bound alone decides.
A program may use at most 64 MiB of HBM per device.

v0:
```python
import jax
import jax.numpy as jnp
from jax import lax
from jax.sharding import PartitionSpec as P

PANEL_BLOCKS = 4


def broadcast(array, axis, root):
    mine = lax.axis_index(axis) == root
    return lax.psum(jnp.where(mine, array, jnp.zeros_like(array)), axis)


def expand(tile, mask):
    row_blocks, col_blocks = mask.shape
    edge_len = tile.shape[0] // row_blocks
    grid = mask.astype(jnp.float32)[:, None, :, None]
    full = jnp.broadcast_to(grid, (row_blocks, edge_len, col_blocks, edge_len)).reshape(tile.shape)
    return tile * full


def times_rows(masked_h, arrived):
    return lax.dot_general(
        masked_h,
        arrived,
        (((1,), (1,)), ((), ())),
        precision=lax.Precision.HIGHEST,
        preferred_element_type=jnp.float32,
    )


def on_device(x_matrix, h_matrix, x_mask, h_mask, panel):
    masked_x = expand(x_matrix, x_mask)
    masked_h = expand(h_matrix, h_mask)
    edge_len = x_matrix.shape[0] // x_mask.shape[0]
    width = PANEL_BLOCKS * edge_len
    band_rows = masked_x.shape[0]
    first = panel[0] * width
    source = first // band_rows
    offset = first % band_rows
    piece = lax.dynamic_slice_in_dim(masked_x, offset, width, 0)
    arrived = broadcast(piece, "row", source)
    partial_value = times_rows(masked_h, arrived)
    column_total = lax.psum(partial_value, "col")
    return lax.psum_scatter(
        lax.dot_general(
            column_total,
            masked_x,
            (((0,), (0,)), ((), ())),
            precision=lax.Precision.HIGHEST,
            preferred_element_type=jnp.float32,
        ),
        "row",
        scatter_dimension=0,
        tiled=True,
    )


def solution(mesh):
    return jax.shard_map(
        on_device,
        mesh=mesh,
        in_specs=(P("row", "col"), P("row", "col"), P("row", "col"), P("row", "col"), P()),
        out_specs=P("row", "col"),
        check_vma=False,
    )
```

profile of v0, /device:TPU:1, one launch (start us, length us, event | category | flops | bytes accessed | tf_op | source)
XLA Modules:
  0.0 414.8 jit_solution(18012232849832946659)
XLA Ops:
  6.5 0.0 all-reduce.3.cloned.1.call-start
  7.2 0.7 convert_element_type.7
  7.9 0.0 copy-start.1
  7.9 0.3 broadcast_in_dim.7
  8.3 1.8 copy-done.1
  10.1 1.5 bitcast_multiply_fusion
  11.6 0.0 copy-start
  11.6 1.9 copy-done
  13.6 0.0 copy-start.3
  13.6 1.6 dynamic-slice_select_fusion
  15.2 0.0 all-reduce.3.cloned.1.call-update
  15.2 0.0 all-reduce.5.cloned.1.call-start
  15.3 0.0 copy-done.3
  15.3 153.1 %all-reduce.3.cloned.1.call-done = f32[512,1024]{1,0:T(8,128)} async-done(((f32[512,1024]{1,0:T(8,128)}), f32[512,1024]{1,0:T(8,128)}) %all-reduce.3.cloned.1.call-update) | async-done | bytes 2097168 | tf_op jit(solution)/shard_map/psum | solution.py:11
  168.3 0.0 copy-start.2
  168.3 0.3 broadcast_in_dim.6
  168.7 1.8 copy-done.2
  170.5 9.9 %fusion = f32[1024,512]{1,0:T(8,128)} fusion(f32[512,1024]{1,0:T(8,128)} %all-reduce.3.cloned.1.call-done, f32[1024,1024]{1,0:T(8,128)S(1)} %copy-done.2, f32[128,8,8,128]{3,2,1,0:T(8,128)S(1)} %bitcast.13), kind=kOutput, calls=%fused_computation.2 | convolution fusion | flops 6443499520 | bytes 12582912 | tf_op jit(solution)/shard_map/dot_general | solution.py:23
  180.4 0.0 all-reduce.5.cloned.1.call-update
  180.4 0.0 reduce-scatter.2.cloned.1.call-start
  180.5 133.7 %all-reduce.5.cloned.1.call-done = f32[1024,512]{1,0:T(8,128)} async-done(((f32[1024,512]{1,0:T(8,128)}), f32[1024,512]{1,0:T(8,128)}) %all-reduce.5.cloned.1.call-update) | async-done | bytes 2097168 | tf_op jit(solution)/shard_map/psum | solution.py:44
  314.2 10.3 %fusion.2 = f32[512,1024]{1,0:T(8,128)} fusion(f32[1024,512]{1,0:T(8,128)} %all-reduce.5.cloned.1.call-done, f32[1024,1024]{1,0:T(8,128)} %copy-done), kind=kOutput, calls=%fused_computation.5 | convolution fusion | flops 6442450944 | bytes 8388608 | tf_op jit(solution)/shard_map/dot_general | solution.py:46
  324.5 0.0 reduce-scatter.2.cloned.1.call-update
  324.5 83.8 %reduce-scatter.2.cloned.1.call-done = f32[32,1024]{1,0:T(8,128)} async-done(((f32[512,1024]{1,0:T(8,128)}), f32[32,1024]{1,0:T(8,128)}) %reduce-scatter.2.cloned.1.call-update) | async-done | bytes 131088 | tf_op jit(solution)/shard_map/reduce_scatter | solution.py:45
  (1 shorter events, 0.0 us)
Async XLA Ops:
  6.5 161.8 %all-reduce.3.cloned.1.call-start = ((), (), s32[]{:S(2)}) async-start(), calls=%async_computation.1 | async-start | bytes 4194304 | tf_op jit(solution)/shard_map/psum | solution.py:11
  7.9 2.2 copy-start.1
  11.6 1.9 copy-start
  13.6 1.7 copy-start.3
  15.2 299.0 %all-reduce.5.cloned.1.call-start = ((), (), s32[]{:S(2)}) async-start(), calls=%async_computation.2 | async-start | bytes 4194304 | tf_op jit(solution)/shard_map/psum | solution.py:44
  168.3 2.2 copy-start.2
  180.4 227.9 %reduce-scatter.2.cloned.1.call-start = ((), (), s32[]{:S(2)}) async-start(), calls=%async_computation.3 | async-start | bytes 2228224 | tf_op jit(solution)/shard_map/reduce_scatter | solution.py:45
Sparse Core Ops, SparseCore 0:
  15.3 152.9 all-reduce.2
  180.5 133.6 all-reduce.4
  324.6 83.6 reduce-scatter.1
where the time goes:
time: 416 us; the launch traced here: 415 us
  waiting for transfers between devices  371 us (89%)
  matrix products  20.1 us (5%)
  between operations  13.8 us (3%)
  local copies, waits for them, and re-layouts  6.29 us (2%)
    psum x1, waiting for transfers between devices, broadcast(): return lax.psum(jnp.where(mine, array, jnp.zeros_like(array)), axis)  153 us
    psum x1, waiting for transfers between devices, on_device(): column_total = lax.psum(partial_value, 'col')  134 us
    reduce_scatter x1, waiting for transfers between devices, on_device(): lax.psum_scatter(lax.dot_general(column_total, masked_x, (((0,), (0,)), (...  83.8 us
    dot_general x1, matrix products, on_device(): lax.dot_general(column_total, masked_x, (((0,), (0,)), ((), ())), precisi...  10.3 us
    dot_general x1, matrix products, times_rows(): lax.dot_general(masked_h, arrived, (((1,), (1,)), ((), ())), precision=la...  9.86 us
  transfers between devices with their start and end apart: 3, of which 3 were waited for; matrix products, arithmetic and copies ran while one was open for 0% of the time, Pallas kernels for 0%

commit v1 on v0

v1 whole, which is shorter than its diff:
```python
import functools

import jax
import jax.numpy as jnp
from jax import lax
from jax.experimental import pallas as pl
from jax.experimental.pallas import tpu as pltpu
from jax.sharding import PartitionSpec as P

MESH = pl.DeviceIdType.MESH
CHUNKS = 4
PANEL = 512
CHIPS = 8
RING = 8
EDGE = 128

DUE = {"A0": 0, "A1": 2, "A2": 6, "A3": 10, "A4": 12, "Z2": 15, "Z3": 18, "Z4": 21, "Z5": 24, "Z6": 27,
       "Z7": 30, "Z8": 33, "Z9": 36, "Z10": 38, "B1": 41, "B2": 45}
APART = 8
PREPARE = {"x_load": -1, "h_prep": 0.5, "x_prep": 11}

CORE_P, DIR_P, AG_P, CORE_R, CORE_O, DIR_O, YX = range(7)
RU, RD, GU, GD = 7, 11, 15, 19
N_SEMS = 23


def order():
    steps = [(t + APART * k, k, name) for k in range(CHUNKS) for name, t in DUE.items()]
    steps += [(t, -1, name) for name, t in PREPARE.items()]
    return [(name, k) for _, k, name in sorted(steps)]


def kernel(x_hbm, h_hbm, xm_ref, hm_ref, panel_ref, out_ref,
           xv, hv, xh, xl, hh, hl, wx, mx, mh, piece, pc, pr, rr, ab, tp, zu1, zd1, zu, zd, yr, tf,
           ob, oc, orv, load_sem, send, recv):
    row, col = lax.axis_index("row"), lax.axis_index("col")
    core, chip = lax.rem(row, 2), lax.div(row, 2)
    z, ylo = lax.rem(col, RING), lax.div(col, RING)
    sib = (row + 1 - 2 * core, col)
    ypart = (row, (1 - ylo) * RING + z)
    up = (row, ylo * RING + lax.rem(z + 1, RING))
    down = (row, ylo * RING + lax.rem(z + RING - 1, RING))

    def peer(d):
        return (lax.rem(chip + d, CHIPS) * 2 + core, col)

    def at_z(d):
        return lax.rem(z + (d + RING) % RING, RING)

    load_x = pltpu.make_async_copy(x_hbm, xv, load_sem.at[0])
    load_h = pltpu.make_async_copy(h_hbm, hv, load_sem.at[1])
    load_x.start()
    load_h.start()

    barrier = pltpu.get_barrier_semaphore()
    friends = [sib, ypart, up, down] + [peer(d) for d in range(1, CHIPS)]
    for friend in friends:
        pl.semaphore_signal(barrier, inc=1, device_id=friend, device_id_type=MESH)

    def remote(src, dst, k, sem, device):
        return pltpu.make_async_remote_copy(
            src_ref=src, dst_ref=dst, send_sem=send.at[k, sem], recv_sem=recv.at[k, sem],
            device_id=device, device_id_type=MESH)

    sent = []

    def push(src, dst, k, sem, device):
        copy = remote(src, dst, k, sem, device)
        copy.start()
        sent.append(copy)

    def spread(mask):
        m = mask.astype(jnp.float32)
        return jnp.concatenate(
            [jnp.broadcast_to(m[:, j:j + 1], (m.shape[0], EDGE)) for j in range(m.shape[1])], axis=1)

    def split(value):
        high = value.astype(jnp.bfloat16)
        return high, (value - high.astype(jnp.float32)).astype(jnp.bfloat16)

    def multiply(chunk, high, low, store, transposed):
        rows = chunk.shape[0]
        a, b = split(chunk)
        ab[0:rows, :] = a
        ab[rows:2 * rows, :] = b
        dims = (((1,), (1 if transposed else 0,)), ((), ()))

        def body(n, carry):
            cols = pl.ds(pl.multiple_of(n * 256, 256), 256)
            wh = high[cols, :] if transposed else high[:, cols]
            wl = low[cols, :] if transposed else low[:, cols]
            first = lax.dot_general(ab[...], wh, dims, preferred_element_type=jnp.float32)
            second = lax.dot_general(ab[0:rows, :], wl, dims, preferred_element_type=jnp.float32)
            store(cols, first[:rows] + (first[rows:] + second))
            return carry

        lax.fori_loop(0, high.shape[0] // 256, body, 0)

    def x_load():
        mx[...] = spread(xm_ref[...])
        s0 = jnp.where(panel_ref[0] == 2 * row, 1.0, 0.0)
        s1 = jnp.where(panel_ref[0] == 2 * row + 1, 1.0, 0.0)
        wx[0] = mx[0:4, :] * s0
        wx[1] = mx[4:8, :] * s1
        load_x.wait()

    def h_prep():
        mh[...] = spread(hm_ref[...])
        load_h.wait()

        def body(b, carry):
            rows = pl.ds(pl.multiple_of(b * EDGE, EDGE), EDGE)
            high, low = split(hv[rows, :] * mh[pl.ds(b, 1), :])
            hh[rows, :] = high
            hl[rows, :] = low
            return carry

        lax.fori_loop(0, 8, body, 0)

    def x_prep():
        def body(b, carry):
            rows = pl.ds(pl.multiple_of(b * EDGE, EDGE), EDGE)
            block = xv[lax.div(b, 4), pl.ds(lax.rem(b, 4) * 2, 2)].reshape(EDGE, 1024)
            high, low = split(block * mx[pl.ds(b, 1), :])
            xh[rows, :] = high
            xl[rows, :] = low
            return carry

        lax.fori_loop(0, 8, body, 0)

    def a0(k):
        for q in range(2):
            for g in range(CHIPS):
                w0, w1 = wx[0, g // 2:g // 2 + 1, :], wx[1, g // 2:g // 2 + 1, :]
                piece[k, q, g] = xv[0, g, q, k] * w0 + xv[1, g, q, k] * w1
        if k == 0:
            pl.semaphore_wait(barrier, len(friends))
        push(piece.at[k, 1 - core], pc.at[k], k, CORE_P, sib)

    def a1(k):
        remote(pc.at[k], pc.at[k], k, CORE_P, sib).wait_recv()
        piece[k, core] = piece[k, core] + pc[k]
        for d in range(1, CHIPS):
            remote(piece.at[k, core, lax.rem(chip + d, CHIPS)], pr.at[k, d - 1], k, DIR_P, peer(d)).start()
        sent.append(remote(pr.at[k], pr.at[k], k, DIR_P, sib))

    def a2(k):
        remote(pr.at[k], pr.at[k], k, DIR_P, sib).wait_recv()
        total = piece[k, core, chip]
        for d in range(CHIPS - 1):
            total = total + pr[k, d]
        rr[k, core, chip] = total
        for d in range(1, CHIPS):
            remote(rr.at[k, core, chip], rr.at[k, core, chip], k, AG_P, peer(d)).start()
        sent.append(remote(pr.at[k], pr.at[k], k, AG_P, sib))

    def a3(k):
        remote(pr.at[k], pr.at[k], k, AG_P, sib).wait_recv()
        push(rr.at[k, core], rr.at[k, core], k, CORE_R, sib)

    def a4(k):
        remote(rr.at[k, core], rr.at[k, 1 - core], k, CORE_R, sib).wait_recv()
        rows = PANEL // CHUNKS

        def store(cols, value):
            tp[k, :, :, cols] = value.reshape(RING, rows // RING, 256)

        multiply(rr[k].reshape(rows, 1024), hh, hl, store, True)
        push(tp.at[k, at_z(4), :, 0:512], zu1.at[k], k, RU, up)
        push(tp.at[k, at_z(4), :, 512:1024], zd1.at[k], k, RD, down)

    def z2(k):
        remote(zu1.at[k], zu1.at[k], k, RU, up).wait_recv()
        tp[k, at_z(3), :, 0:512] = tp[k, at_z(3), :, 0:512] + zu1[k]
        push(tp.at[k, at_z(3)], zu.at[k, 0], k, RU + 1, up)
        remote(zd1.at[k], zd1.at[k], k, RD, down).wait_recv()
        tp[k, at_z(-3), :, 512:1024] = tp[k, at_z(-3), :, 512:1024] + zd1[k]
        push(tp.at[k, at_z(-3)], zd.at[k, 0], k, RD + 1, down)

    def z_add(k, s):
        remote(zu.at[k, s], zu.at[k, s], k, RU + 1 + s, up).wait_recv()
        tp[k, at_z(2 - s)] = tp[k, at_z(2 - s)] + zu[k, s]
        push(tp.at[k, at_z(2 - s)], zu.at[k, s + 1], k, RU + 2 + s, up)
        remote(zd.at[k, s], zd.at[k, s], k, RD + 1 + s, down).wait_recv()
        tp[k, at_z(s - 2)] = tp[k, at_z(s - 2)] + zd[k, s]
        push(tp.at[k, at_z(s - 2)], zd.at[k, s + 1], k, RD + 2 + s, down)

    def z5(k):
        remote(zu.at[k, 2], zu.at[k, 2], k, RU + 3, up).wait_recv()
        remote(zd.at[k, 2], zd.at[k, 2], k, RD + 3, down).wait_recv()
        tp[k, z] = tp[k, z] + (zu[k, 2] + zd[k, 2])
        push(tp.at[k, z], yr.at[k], k, YX, ypart)

    def z6(k):
        remote(yr.at[k], yr.at[k], k, YX, ypart).wait_recv()
        tf[k, z] = tp[k, z] + yr[k]
        push(tf.at[k, z], tf.at[k, z], k, GU, up)
        push(tf.at[k, z], tf.at[k, z], k, GD, down)

    def z_pass(k, s):
        below, above = at_z(-s), at_z(s)
        remote(tf.at[k, below], tf.at[k, below], k, GU + s - 1, up).wait_recv()
        if s < 3:
            push(tf.at[k, below], tf.at[k, below], k, GU + s, up)
        else:
            push(tf.at[k, below, :, 0:512], tf.at[k, below, :, 0:512], k, GU + s, up)
        remote(tf.at[k, above], tf.at[k, above], k, GD + s - 1, down).wait_recv()
        if s < 3:
            push(tf.at[k, above], tf.at[k, above], k, GD + s, down)
        else:
            push(tf.at[k, above, :, 512:1024], tf.at[k, above, :, 512:1024], k, GD + s, down)

    def z10(k):
        far = at_z(4)
        remote(tf.at[k, far, :, 0:512], tf.at[k, far, :, 0:512], k, GU + 3, up).wait_recv()
        remote(tf.at[k, far, :, 512:1024], tf.at[k, far, :, 512:1024], k, GD + 3, down).wait_recv()
        rows = PANEL // CHUNKS

        def store(cols, value):
            ob[k, :, :, :, cols] = value.reshape(2, CHIPS, rows // 16, 256)

        multiply(tf[k].reshape(rows, 1024), xh, xl, store, False)
        push(ob.at[k, 1 - core], oc.at[k], k, CORE_O, sib)

    def b1(k):
        remote(oc.at[k], oc.at[k], k, CORE_O, sib).wait_recv()
        ob[k, core] = ob[k, core] + oc[k]
        for d in range(1, CHIPS):
            remote(ob.at[k, core, lax.rem(chip + d, CHIPS)], orv.at[k, d - 1], k, DIR_O, peer(d)).start()
        sent.append(remote(orv.at[k], orv.at[k], k, DIR_O, sib))

    def b2(k):
        remote(orv.at[k], orv.at[k], k, DIR_O, sib).wait_recv()
        total = ob[k, core, chip]
        for d in range(CHIPS - 1):
            total = total + orv[k, d]
        out_ref[k] = total

    stages = {
        "A0": a0, "A1": a1, "A2": a2, "A3": a3, "A4": a4, "Z2": z2,
        "Z3": lambda k: z_add(k, 0), "Z4": lambda k: z_add(k, 1), "Z5": z5, "Z6": z6,
        "Z7": lambda k: z_pass(k, 1), "Z8": lambda k: z_pass(k, 2), "Z9": lambda k: z_pass(k, 3),
        "Z10": z10, "B1": b1, "B2": b2,
        "x_load": lambda k: x_load(), "h_prep": lambda k: h_prep(), "x_prep": lambda k: x_prep(),
    }
    for name, k in order():
        stages[name](k)
    for copy in sent:
        copy.wait_send()


def on_device(x_matrix, h_matrix, x_mask, h_mask, panel):
    n, slab = x_matrix.shape[0], 32 // CHUNKS
    group = PANEL // CHUNKS // RING
    f32, bf16 = jnp.float32, jnp.bfloat16
    vmem, hbm = pl.BlockSpec(memory_space=pltpu.VMEM), pl.BlockSpec(memory_space=pl.ANY)
    out = pl.pallas_call(
        kernel,
        out_shape=jax.ShapeDtypeStruct((CHUNKS, slab, n), f32),
        in_specs=[hbm, hbm, vmem, vmem, pl.BlockSpec(memory_space=pltpu.SMEM)],
        out_specs=vmem,
        scratch_shapes=[
            pltpu.VMEM((2, CHIPS, 2, CHUNKS, slab, n), f32),
            pltpu.VMEM((n, n), f32),
            pltpu.VMEM((n, n), bf16), pltpu.VMEM((n, n), bf16),
            pltpu.VMEM((n, n), bf16), pltpu.VMEM((n, n), bf16),
            pltpu.VMEM((2, 4, n), f32), pltpu.VMEM((8, n), f32), pltpu.VMEM((8, n), f32),
            pltpu.VMEM((CHUNKS, 2, CHIPS, slab, n), f32),
            pltpu.VMEM((CHUNKS, CHIPS, slab, n), f32),
            pltpu.VMEM((CHUNKS, CHIPS - 1, slab, n), f32),
            pltpu.VMEM((CHUNKS, 2, CHIPS, slab, n), f32),
            pltpu.VMEM((2 * PANEL // CHUNKS, n), bf16),
            pltpu.VMEM((CHUNKS, RING, group, n), f32),
            pltpu.VMEM((CHUNKS, group, n // 2), f32), pltpu.VMEM((CHUNKS, group, n // 2), f32),
            pltpu.VMEM((CHUNKS, 3, group, n), f32), pltpu.VMEM((CHUNKS, 3, group, n), f32),
            pltpu.VMEM((CHUNKS, group, n), f32),
            pltpu.VMEM((CHUNKS, RING, group, n), f32),
            pltpu.VMEM((CHUNKS, 2, CHIPS, slab, n), f32),
            pltpu.VMEM((CHUNKS, CHIPS, slab, n), f32),
            pltpu.VMEM((CHUNKS, CHIPS - 1, slab, n), f32),
            pltpu.SemaphoreType.DMA((2,)),
            pltpu.SemaphoreType.DMA((CHUNKS, N_SEMS)),
            pltpu.SemaphoreType.DMA((CHUNKS, N_SEMS)),
        ],
        compiler_params=pltpu.CompilerParams(
            collective_id=0, has_side_effects=True, vmem_limit_bytes=56 * 1024 * 1024),
    )(x_matrix.reshape(2, CHIPS, 2, CHUNKS, slab, n), h_matrix, x_mask, h_mask, panel)
    return out.reshape(32, n)


def solution(mesh):
    return jax.shard_map(
        on_device,
        mesh=mesh,
        in_specs=(P("row", "col"), P("row", "col"), P("row", "col"), P("row", "col"), P()),
        out_specs=P("row", "col"),
        check_vma=False,
    )
```

time: 416 us -> 116 us (0.28)
  waiting for transfers between devices: 371 us -> 0 us
  Pallas kernels: 0 us -> 114 us
  matrix products: 20.1 us -> 0 us
  between operations: 13.8 us -> 0.66 us
  local copies, waits for them, and re-layouts: 6.29 us -> 1.57 us
    psum x2 -> x0, waiting for transfers between devices: 287 us -> none  [the longest x1 153 us: broadcast(): return lax.psum(jnp.where(mine, array, jnp.zeros_like(array)), axis)]
    pallas_call x0 -> x1, Pallas kernels: none -> 114 us  [on_device(): pl.pallas_call(kernel, out_shape=jax.ShapeDtypeStruct((CHUNKS, slab, n),...]
    reduce_scatter x1 -> x0, waiting for transfers between devices: 83.8 us -> none  [on_device(): lax.psum_scatter(lax.dot_general(column_total, masked_x, (((0,), (0,)), (...]
    dot_general x2 -> x0, matrix products: 20.1 us -> none  [the longest x1 10.3 us: on_device(): lax.dot_general(column_total, masked_x, (((0,), (0,)), ((), ())), precisi...]
  transfers between devices with their start and end apart: 3 -> 0, of which waited for: 3 -> 0; matrix products, arithmetic and copies ran while one was open for 0% -> 0% of each run, Pallas kernels for 0% -> 0%
where the time goes in v1:
time: 116 us
  Pallas kernels  114 us (98%)
  local copies, waits for them, and re-layouts  1.57 us (1%)
    pallas_call x1, Pallas kernels, on_device(): pl.pallas_call(kernel, out_shape=jax.ShapeDtypeStruct((CHUNKS, slab, n),...  114 us

profile of v1, /device:TPU:1, one launch (start us, length us, event | category | flops | bytes accessed | tf_op | source)
XLA Modules:
  0.0 115.7 jit_solution(3294544282176117460)
XLA Ops:
  0.7 113.5 %shard_map.55 = f32[4,8,1024]{2,1,0:T(8,128)} custom-call(f32[2,8,2,4,8,1024]{5,4,3,2,1,0:T(8,128)} %bitcast.2, f32[1024,1024]{1,0:T(8,128)} %h_hbm.1, s32[8,8]{1,0:T(8,128)} %xm_ref.1, s32[8,8]{1,0:T(8,128)} %hm_ref.1, s32[1]{0:T(128)S(6)} %copy.7.panel_ref), custom_call_target="tpu_custom_call" | custom-call | tf_op jit(solution)/shard_map/pallas_call | solution.py:257
  114.2 1.6 %copy.8 = f32[32,1024]{1,0:T(8,128)} copy(f32[32,1024]{1,0:T(8,128)} %bitcast.3) | data formatting | bytes 262144

commit v2 on v1

v2 whole, which is shorter than its diff:
```python
import functools

import jax
import jax.numpy as jnp
from jax import lax
from jax.experimental import pallas as pl
from jax.experimental.pallas import tpu as pltpu
from jax.sharding import PartitionSpec as P

MESH = pl.DeviceIdType.MESH
CHUNKS = 4
PANEL = 512
ROWS = PANEL // CHUNKS
CHIPS = 8
RING = 8
EDGE = 128

ORDER = (
    ("x_load", 0), ("A0", 0), ("A0", 1), ("A1", 0), ("A0", 2), ("A1", 1), ("A1", 2), ("A0", 3), ("h_prep", 0),
    ("A2", 0), ("A1", 3), ("x_prep", 0), ("A2", 2), ("A2", 1), ("A3", 0), ("A4", 0), ("A4b", 0), ("A2", 3),
    ("Z2", 0), ("A3", 2), ("A4", 2), ("A3", 1), ("A4b", 2), ("Z3", 0), ("A4", 1), ("A4b", 1), ("Z2", 2),
    ("A3", 3), ("A4", 3), ("Z2", 1), ("A4b", 3), ("Z3", 2), ("Z4", 0), ("Z2", 3), ("Z3", 1), ("Z4", 2), ("Z6", 0),
    ("Z3", 3), ("Z4", 1), ("Z6", 2), ("Z7", 0), ("P1", 0), ("Z4", 3), ("Z6", 1), ("Z7", 2), ("P1", 2), ("Z8", 0),
    ("P2", 0), ("Z6", 3), ("Z7", 1), ("P1", 1), ("Z8", 2), ("P2", 2), ("Z9", 0), ("P3", 0), ("Z7", 3), ("P1", 3),
    ("Z8", 1), ("P2", 1), ("Z9", 2), ("P3", 2), ("Z11", 0), ("Z8", 3), ("P2", 3), ("B1", 0), ("Z9", 1), ("P3", 1),
    ("Z11", 2), ("B1", 2), ("Z9", 3), ("P3", 3), ("Z11", 1), ("B1", 1), ("Z11", 3), ("B1", 3), ("B2", 1),
    ("B2", 2), ("B2", 0), ("B2", 3),
)

CORE_P, DIR_P, AG_P, CORE_R, CORE_O, DIR_O, LAST, FIRST = range(8)
RU, RD, GU, GD = 8, 11, 14, 17
N_SEMS = 20


def kernel(x_hbm, h_hbm, xm_ref, hm_ref, panel_ref, out_ref,
           xv, hv, xh, xl, hh, hl, wx, mx, mh, piece, pc, pr, rr, ab, tb, tp, zu1, zd1, zu, zd, zl, tf,
           ob, oc, orv, load_sem, send, recv):
    row, col = lax.axis_index("row"), lax.axis_index("col")
    core, chip = lax.rem(row, 2), lax.div(row, 2)
    z, ylo = lax.rem(col, RING), lax.div(col, RING)
    sib = (row + 1 - 2 * core, col)
    other = 1 - ylo
    ypart = (row, other * RING + z)
    z_up, z_down = lax.rem(z + 1, RING), lax.rem(z + RING - 1, RING)
    up, up_other = (row, ylo * RING + z_up), (row, other * RING + z_up)
    down, down_other = (row, ylo * RING + z_down), (row, other * RING + z_down)
    around = [up, down, up_other, down_other, ypart]

    def peer(d):
        return (lax.rem(chip + d, CHIPS) * 2 + core, col)

    def at_z(d):
        return lax.rem(z + (d + RING) % RING, RING)

    load_x = pltpu.make_async_copy(x_hbm, xv, load_sem.at[0])
    load_h = pltpu.make_async_copy(h_hbm, hv, load_sem.at[1])
    load_x.start()

    barrier = pltpu.get_barrier_semaphore()
    friends = [sib] + around + [peer(d) for d in range(1, CHIPS)]
    for friend in friends:
        pl.semaphore_signal(barrier, inc=1, device_id=friend, device_id_type=MESH)

    def remote(src, dst, k, sem, device):
        return pltpu.make_async_remote_copy(
            src_ref=src, dst_ref=dst, send_sem=send.at[k, sem], recv_sem=recv.at[k, sem],
            device_id=device, device_id_type=MESH)

    sent = []

    def push(src, dst, k, sem, device):
        copy = remote(src, dst, k, sem, device)
        copy.start()
        sent.append(copy)

    def spread(mask):
        m = mask.astype(jnp.float32)
        return jnp.concatenate(
            [jnp.broadcast_to(m[:, j:j + 1], (m.shape[0], EDGE)) for j in range(m.shape[1])], axis=1)

    def split(value):
        high = value.astype(jnp.bfloat16)
        return high, (value - high.astype(jnp.float32)).astype(jnp.bfloat16)

    def product_one(k, step):
        far = lax.div(at_z(4), 2)
        turn = 1 - 2 * lax.rem(z + 1, 2)
        pair = lax.rem(far + (0, 4 + turn, 4 - turn, 2)[step], 4)
        rows = pl.ds(pl.multiple_of(pair * 256, 256), 256)
        dims = (((1,), (1,)), ((), ()))
        first = lax.dot_general(ab[k], hh[rows, :], dims, preferred_element_type=jnp.float32)
        second = lax.dot_general(ab[k, 0:ROWS, :], hl[rows, :], dims, preferred_element_type=jnp.float32)
        value = first[:ROWS] + (first[ROWS:] + second)
        tp[k, 2 * pair] = value[:, :EDGE].reshape(2, ROWS // 2, EDGE)
        tp[k, 2 * pair + 1] = value[:, EDGE:].reshape(2, ROWS // 2, EDGE)

    def product_two(k, step):
        turn = 1 - 2 * lax.rem(z + 1, 2)
        pair = lax.rem(lax.div(z, 2) + (0, 4 + turn, 4 - turn, 2)[step], 4)
        for half in range(2):
            a, b = split(tf[k, 2 * pair + half].reshape(ROWS, EDGE))
            tb[0:ROWS, half * EDGE:(half + 1) * EDGE] = a
            tb[ROWS:, half * EDGE:(half + 1) * EDGE] = b
        rows = pl.ds(pl.multiple_of(pair * 256, 256), 256)
        for n in range(0, 1024, 256):
            first = jnp.dot(tb[...], xh[rows, n:n + 256], preferred_element_type=jnp.float32)
            second = jnp.dot(tb[0:ROWS, :], xl[rows, n:n + 256], preferred_element_type=jnp.float32)
            value = (first[:ROWS] + (first[ROWS:] + second)).reshape(2, CHIPS, ROWS // 16, 256)
            ob[k, :, :, :, n:n + 256] = value if step == 0 else ob[k, :, :, :, n:n + 256] + value

    def x_load():
        mx[...] = spread(xm_ref[...])
        s0 = jnp.where(panel_ref[0] == 2 * row, 1.0, 0.0)
        s1 = jnp.where(panel_ref[0] == 2 * row + 1, 1.0, 0.0)
        wx[0] = mx[0:4, :] * s0
        wx[1] = mx[4:8, :] * s1
        load_x.wait()
        load_h.start()

    def h_prep():
        mh[...] = spread(hm_ref[...])
        load_h.wait()

        def body(b, carry):
            rows = pl.ds(pl.multiple_of(b * EDGE, EDGE), EDGE)
            high, low = split(hv[rows, :] * mh[pl.ds(b, 1), :])
            hh[rows, :] = high
            hl[rows, :] = low
            return carry

        lax.fori_loop(0, 8, body, 0)

    def x_prep():
        def body(b, carry):
            rows = pl.ds(pl.multiple_of(b * EDGE, EDGE), EDGE)
            block = xv[lax.div(b, 4), pl.ds(lax.rem(b, 4) * 2, 2)].reshape(EDGE, 1024)
            high, low = split(block * mx[pl.ds(b, 1), :])
            xh[rows, :] = high
            xl[rows, :] = low
            return carry

        lax.fori_loop(0, 8, body, 0)

    def a0(k):
        for q in range(2):
            for g in range(CHIPS):
                w0, w1 = wx[0, g // 2:g // 2 + 1, :], wx[1, g // 2:g // 2 + 1, :]
                piece[k, q, g] = xv[0, g, q, k] * w0 + xv[1, g, q, k] * w1
        if not sent:
            pl.semaphore_wait(barrier, len(friends))
        push(piece.at[k, 1 - core], pc.at[k], k, CORE_P, sib)

    def a1(k):
        remote(pc.at[k], pc.at[k], k, CORE_P, sib).wait_recv()
        piece[k, core] = piece[k, core] + pc[k]
        for d in range(1, CHIPS):
            remote(piece.at[k, core, lax.rem(chip + d, CHIPS)], pr.at[k, d - 1], k, DIR_P, peer(d)).start()
        sent.append(remote(pr.at[k], pr.at[k], k, DIR_P, sib))

    def a2(k):
        remote(pr.at[k], pr.at[k], k, DIR_P, sib).wait_recv()
        total = piece[k, core, chip]
        for d in range(CHIPS - 1):
            total = total + pr[k, d]
        rr[k, core, chip] = total
        for d in range(1, CHIPS):
            remote(rr.at[k, core, chip], rr.at[k, core, chip], k, AG_P, peer(d)).start()
        sent.append(remote(pr.at[k], pr.at[k], k, AG_P, sib))

    def a3(k):
        remote(pr.at[k], pr.at[k], k, AG_P, sib).wait_recv()
        push(rr.at[k, core], rr.at[k, core], k, CORE_R, sib)

    def a4(k):
        remote(rr.at[k, core], rr.at[k, 1 - core], k, CORE_R, sib).wait_recv()
        high, low = split(rr[k].reshape(ROWS, 1024))
        ab[k, 0:ROWS, :] = high
        ab[k, ROWS:, :] = low
        product_one(k, 0)
        push(tp.at[k, at_z(4), 0], zu1.at[k], k, RU, up)
        push(tp.at[k, at_z(4), 1], zd1.at[k], k, RD, down)

    def a4b(k):
        for step in (1, 2, 3):
            product_one(k, step)
        remote(tp.at[k, z, other], zl.at[k, 4], k, LAST, ypart).start()

    def z2(k):
        remote(zu1.at[k], zu1.at[k], k, RU, up).wait_recv()
        tp[k, at_z(3), 0] = tp[k, at_z(3), 0] + zu1[k]
        push(tp.at[k, at_z(3)], zu.at[k, 0], k, RU + 1, up)
        remote(zd1.at[k], zd1.at[k], k, RD, down).wait_recv()
        tp[k, at_z(-3), 1] = tp[k, at_z(-3), 1] + zd1[k]
        push(tp.at[k, at_z(-3)], zd.at[k, 0], k, RD + 1, down)

    def z3(k):
        remote(zu.at[k, 0], zu.at[k, 0], k, RU + 1, up).wait_recv()
        tp[k, at_z(2)] = tp[k, at_z(2)] + zu[k, 0]
        push(tp.at[k, at_z(2)], zu.at[k, 1], k, RU + 2, up)
        remote(zd.at[k, 0], zd.at[k, 0], k, RD + 1, down).wait_recv()
        tp[k, at_z(-2)] = tp[k, at_z(-2)] + zd[k, 0]
        push(tp.at[k, at_z(-2)], zd.at[k, 1], k, RD + 2, down)

    def z4(k):
        remote(zu.at[k, 1], zu.at[k, 1], k, RU + 2, up).wait_recv()
        tp[k, z_up] = tp[k, z_up] + zu[k, 1]
        remote(tp.at[k, z_up, other], zl.at[k, 2], k, LAST, up_other).start()
        remote(tp.at[k, z_up, ylo], zl.at[k, 0], k, LAST, up).start()
        remote(zd.at[k, 1], zd.at[k, 1], k, RD + 2, down).wait_recv()
        tp[k, z_down] = tp[k, z_down] + zd[k, 1]
        remote(tp.at[k, z_down, other], zl.at[k, 3], k, LAST, down_other).start()
        remote(tp.at[k, z_down, ylo], zl.at[k, 1], k, LAST, down).start()
        sent.append(remote(zl.at[k], zl.at[k], k, LAST, up))

    def z6(k):
        remote(zl.at[k], zl.at[k], k, LAST, up).wait_recv()
        total = tp[k, z, ylo]
        for d in range(5):
            total = total + zl[k, d]
        tf[k, z, ylo] = total
        for device in (up_other, down_other, up, down, ypart):
            remote(tf.at[k, z, ylo], tf.at[k, z, ylo], k, FIRST, device).start()
        sent.append(remote(zl.at[k], zl.at[k], k, FIRST, up))

    def z7(k):
        remote(zl.at[k], zl.at[k], k, FIRST, up).wait_recv()
        push(tf.at[k, z_down], tf.at[k, z_down], k, GU, up)
        push(tf.at[k, z_up], tf.at[k, z_up], k, GD, down)

    def z8(k):
        below, above = at_z(-2), at_z(2)
        remote(tf.at[k, below], tf.at[k, below], k, GU, up).wait_recv()
        push(tf.at[k, below], tf.at[k, below], k, GU + 1, up)
        remote(tf.at[k, above], tf.at[k, above], k, GD, down).wait_recv()
        push(tf.at[k, above], tf.at[k, above], k, GD + 1, down)

    def z9(k):
        below, above = at_z(-3), at_z(3)
        remote(tf.at[k, below], tf.at[k, below], k, GU + 1, up).wait_recv()
        push(tf.at[k, below, 0], tf.at[k, below, 0], k, GU + 2, up)
        remote(tf.at[k, above], tf.at[k, above], k, GD + 1, down).wait_recv()
        push(tf.at[k, above, 1], tf.at[k, above, 1], k, GD + 2, down)

    def z11(k):
        far = at_z(4)
        remote(tf.at[k, far, 0], tf.at[k, far, 0], k, GU + 2, up).wait_recv()
        remote(tf.at[k, far, 1], tf.at[k, far, 1], k, GD + 2, down).wait_recv()
        product_two(k, 3)
        push(ob.at[k, 1 - core], oc.at[k], k, CORE_O, sib)

    def b1(k):
        remote(oc.at[k], oc.at[k], k, CORE_O, sib).wait_recv()
        ob[k, core] = ob[k, core] + oc[k]
        for d in range(1, CHIPS):
            remote(ob.at[k, core, lax.rem(chip + d, CHIPS)], orv.at[k, d - 1], k, DIR_O, peer(d)).start()
        sent.append(remote(orv.at[k], orv.at[k], k, DIR_O, sib))

    def b2(k):
        remote(orv.at[k], orv.at[k], k, DIR_O, sib).wait_recv()
        total = ob[k, core, chip]
        for d in range(CHIPS - 1):
            total = total + orv[k, d]
        out_ref[k] = total

    stages = {
        "A0": a0, "A1": a1, "A2": a2, "A3": a3, "A4": a4, "A4b": a4b, "Z2": z2, "Z3": z3, "Z4": z4, "Z6": z6,
        "Z7": z7, "P1": lambda k: product_two(k, 0), "Z8": z8, "P2": lambda k: product_two(k, 1),
        "Z9": z9, "P3": lambda k: product_two(k, 2), "Z11": z11, "B1": b1, "B2": b2,
        "x_load": lambda k: x_load(), "h_prep": lambda k: h_prep(), "x_prep": lambda k: x_prep(),
    }
    for name, k in ORDER:
        stages[name](k)
    for copy in sent:
        copy.wait_send()


def on_device(x_matrix, h_matrix, x_mask, h_mask, panel):
    n, slab = x_matrix.shape[0], 32 // CHUNKS
    part = (ROWS // 2, EDGE)
    f32, bf16 = jnp.float32, jnp.bfloat16
    vmem, hbm = pl.BlockSpec(memory_space=pltpu.VMEM), pl.BlockSpec(memory_space=pl.ANY)
    out = pl.pallas_call(
        kernel,
        out_shape=jax.ShapeDtypeStruct((CHUNKS, slab, n), f32),
        in_specs=[hbm, hbm, vmem, vmem, pl.BlockSpec(memory_space=pltpu.SMEM)],
        out_specs=vmem,
        scratch_shapes=[
            pltpu.VMEM((2, CHIPS, 2, CHUNKS, slab, n), f32),
            pltpu.VMEM((n, n), f32),
            pltpu.VMEM((n, n), bf16), pltpu.VMEM((n, n), bf16),
            pltpu.VMEM((n, n), bf16), pltpu.VMEM((n, n), bf16),
            pltpu.VMEM((2, 4, n), f32), pltpu.VMEM((8, n), f32), pltpu.VMEM((8, n), f32),
            pltpu.VMEM((CHUNKS, 2, CHIPS, slab, n), f32),
            pltpu.VMEM((CHUNKS, CHIPS, slab, n), f32),
            pltpu.VMEM((CHUNKS, CHIPS - 1, slab, n), f32),
            pltpu.VMEM((CHUNKS, 2, CHIPS, slab, n), f32),
            pltpu.VMEM((CHUNKS, 2 * ROWS, n), bf16), pltpu.VMEM((2 * ROWS, 2 * EDGE), bf16),
            pltpu.VMEM((CHUNKS, RING, 2, *part), f32),
            pltpu.VMEM((CHUNKS, *part), f32), pltpu.VMEM((CHUNKS, *part), f32),
            pltpu.VMEM((CHUNKS, 2, 2, *part), f32), pltpu.VMEM((CHUNKS, 2, 2, *part), f32),
            pltpu.VMEM((CHUNKS, 5, *part), f32),
            pltpu.VMEM((CHUNKS, RING, 2, *part), f32),
            pltpu.VMEM((CHUNKS, 2, CHIPS, slab, n), f32),
            pltpu.VMEM((CHUNKS, CHIPS, slab, n), f32),
            pltpu.VMEM((CHUNKS, CHIPS - 1, slab, n), f32),
            pltpu.SemaphoreType.DMA((2,)),
            pltpu.SemaphoreType.DMA((CHUNKS, N_SEMS)),
            pltpu.SemaphoreType.DMA((CHUNKS, N_SEMS)),
        ],
        compiler_params=pltpu.CompilerParams(
            collective_id=0, has_side_effects=True, vmem_limit_bytes=56 * 1024 * 1024),
    )(x_matrix.reshape(2, CHIPS, 2, CHUNKS, slab, n), h_matrix, x_mask, h_mask, panel)
    return out.reshape(32, n)


def solution(mesh):
    return jax.shard_map(
        on_device,
        mesh=mesh,
        in_specs=(P("row", "col"), P("row", "col"), P("row", "col"), P("row", "col"), P()),
        out_specs=P("row", "col"),
        check_vma=False,
    )
```

time: 116 us -> 92.6 us (0.80)
  Pallas kernels: 114 us -> 90.2 us
    pallas_call x1, Pallas kernels: 114 us -> 90.2 us  [on_device(): pl.pallas_call(kernel, out_shape=jax.ShapeDtypeStruct((CHUNKS, slab, n),...]
where the time goes in v2:
time: 92.6 us; the launch traced here: 92.5 us
  Pallas kernels  90.2 us (97%)
  local copies, waits for them, and re-layouts  1.57 us (2%)
    pallas_call x1, Pallas kernels, on_device(): pl.pallas_call(kernel, out_shape=jax.ShapeDtypeStruct((CHUNKS, slab, n),...  90.2 us

profile of v2, /device:TPU:1, one launch (start us, length us, event | category | flops | bytes accessed | tf_op | source)
XLA Modules:
  0.0 92.5 jit_solution(4845041554349390493)
XLA Ops:
  0.7 90.2 %shard_map.55 = f32[4,8,1024]{2,1,0:T(8,128)} custom-call(f32[2,8,2,4,8,1024]{5,4,3,2,1,0:T(8,128)} %bitcast.2, f32[1024,1024]{1,0:T(8,128)} %h_hbm.1, s32[8,8]{1,0:T(8,128)} %xm_ref.1, s32[8,8]{1,0:T(8,128)} %hm_ref.1, s32[1]{0:T(128)S(6)} %copy.7.panel_ref), custom_call_target="tpu_custom_call" | custom-call | tf_op jit(solution)/shard_map/pallas_call | solution.py:282
  90.9 1.6 %copy.8 = f32[32,1024]{1,0:T(8,128)} copy(f32[32,1024]{1,0:T(8,128)} %bitcast.3) | data formatting | bytes 262144

commit v3 on v2

--- a/solution.py
+++ b/solution.py
@@ -16,24 +16,24 @@
 EDGE = 128
 
 ORDER = (
-    ("x_load", 0), ("A0", 0), ("A0", 1), ("A1", 0), ("A0", 2), ("A1", 1), ("A1", 2), ("A0", 3), ("h_prep", 0),
-    ("A2", 0), ("A1", 3), ("x_prep", 0), ("A2", 2), ("A2", 1), ("A3", 0), ("A4", 0), ("A4b", 0), ("A2", 3),
-    ("Z2", 0), ("A3", 2), ("A4", 2), ("A3", 1), ("A4b", 2), ("Z3", 0), ("A4", 1), ("A4b", 1), ("Z2", 2),
-    ("A3", 3), ("A4", 3), ("Z2", 1), ("A4b", 3), ("Z3", 2), ("Z4", 0), ("Z2", 3), ("Z3", 1), ("Z4", 2), ("Z6", 0),
-    ("Z3", 3), ("Z4", 1), ("Z6", 2), ("Z7", 0), ("P1", 0), ("Z4", 3), ("Z6", 1), ("Z7", 2), ("P1", 2), ("Z8", 0),
-    ("P2", 0), ("Z6", 3), ("Z7", 1), ("P1", 1), ("Z8", 2), ("P2", 2), ("Z9", 0), ("P3", 0), ("Z7", 3), ("P1", 3),
-    ("Z8", 1), ("P2", 1), ("Z9", 2), ("P3", 2), ("Z11", 0), ("Z8", 3), ("P2", 3), ("B1", 0), ("Z9", 1), ("P3", 1),
-    ("Z11", 2), ("B1", 2), ("Z9", 3), ("P3", 3), ("Z11", 1), ("B1", 1), ("Z11", 3), ("B1", 3), ("B2", 1),
-    ("B2", 2), ("B2", 0), ("B2", 3),
+    ("x_load", 0), ("A0", 2), ("A0", 3), ("A0", 1), ("A1", 2), ("A1", 3), ("A1", 1), ("A0", 0), ("A1", 0),
+    ("A2", 2), ("A2", 3), ("A2", 1), ("h_prep", 0), ("A2", 0), ("x_prep", 0), ("A3", 2), ("A4", 2), ("A4b", 2),
+    ("A3", 3), ("A4", 3), ("Z2", 2), ("A3", 1), ("A4b", 3), ("A4", 1), ("A4b", 1), ("A3", 0), ("Z2", 3),
+    ("Z3", 2), ("A4", 0), ("Z2", 1), ("A4b", 0), ("Z3", 3), ("Z4", 2), ("Z2", 0), ("Z3", 1), ("Z4", 3), ("Z6", 2),
+    ("Z3", 0), ("Z4", 1), ("Z6", 3), ("Z7", 2), ("Z4", 0), ("Z6", 1), ("Z7", 3), ("Z8", 2), ("P1", 2), ("Z6", 0),
+    ("Z7", 1), ("Z8", 3), ("P1", 3), ("Z9", 2), ("P2", 2), ("Z7", 0), ("P3", 2), ("Z8", 1), ("P1", 1), ("Z11", 2),
+    ("Z9", 3), ("P2", 3), ("P3", 3), ("B1", 2), ("Z8", 0), ("P1", 0), ("Z9", 1), ("P2", 1), ("P3", 1), ("Z11", 3),
+    ("B1", 3), ("Z9", 0), ("P2", 0), ("Z11", 1), ("B2", 2), ("B1", 1), ("P3", 0), ("Z11", 0), ("B1", 0),
+    ("B2", 3), ("B2", 0), ("B2", 1),
 )
 
-CORE_P, DIR_P, AG_P, CORE_R, CORE_O, DIR_O, LAST, FIRST = range(8)
-RU, RD, GU, GD = 8, 11, 14, 17
-N_SEMS = 20
+CORE_P, DIR_P, AG_P, CORE_R, CORE_O, DIR_O, OWN, HALF_U, HALF_D, LAST, FIRST, NEAR, PASS_U, PASS_D = range(14)
+RU, RD, GU, GD = 14, 16, 18, 20
+N_SEMS = 22
 
 
 def kernel(x_hbm, h_hbm, xm_ref, hm_ref, panel_ref, out_ref,
-           xv, hv, xh, xl, hh, hl, wx, mx, mh, piece, pc, pr, rr, ab, tb, tp, zu1, zd1, zu, zd, zl, tf,
+           xv, hv, xh, xl, hh, hl, wx, mx, mh, piece, pc, pr, rr, ab, tb, tp, zu1, zd1, zu, zd, zhu, zhd, zl, yo, tf,
            ob, oc, orv, load_sem, send, recv):
     row, col = lax.axis_index("row"), lax.axis_index("col")
     core, chip = lax.rem(row, 2), lax.div(row, 2)
@@ -183,68 +183,81 @@
     def a4b(k):
         for step in (1, 2, 3):
             product_one(k, step)
-        remote(tp.at[k, z, other], zl.at[k, 4], k, LAST, ypart).start()
+        for slot, owner in enumerate((z_up, z_down, z)):
+            remote(tp.at[k, owner, other], yo.at[k, slot], k, OWN, ypart).start()
+        sent.append(remote(yo.at[k], yo.at[k], k, OWN, ypart))
 
     def z2(k):
         remote(zu1.at[k], zu1.at[k], k, RU, up).wait_recv()
         tp[k, at_z(3), 0] = tp[k, at_z(3), 0] + zu1[k]
-        push(tp.at[k, at_z(3)], zu.at[k, 0], k, RU + 1, up)
+        push(tp.at[k, at_z(3)], zu.at[k], k, RU + 1, up)
         remote(zd1.at[k], zd1.at[k], k, RD, down).wait_recv()
         tp[k, at_z(-3), 1] = tp[k, at_z(-3), 1] + zd1[k]
-        push(tp.at[k, at_z(-3)], zd.at[k, 0], k, RD + 1, down)
+        push(tp.at[k, at_z(-3)], zd.at[k], k, RD + 1, down)
 
     def z3(k):
-        remote(zu.at[k, 0], zu.at[k, 0], k, RU + 1, up).wait_recv()
-        tp[k, at_z(2)] = tp[k, at_z(2)] + zu[k, 0]
-        push(tp.at[k, at_z(2)], zu.at[k, 1], k, RU + 2, up)
-        remote(zd.at[k, 0], zd.at[k, 0], k, RD + 1, down).wait_recv()
-        tp[k, at_z(-2)] = tp[k, at_z(-2)] + zd[k, 0]
-        push(tp.at[k, at_z(-2)], zd.at[k, 1], k, RD + 2, down)
+        remote(zu.at[k], zu.at[k], k, RU + 1, up).wait_recv()
+        tp[k, at_z(2)] = tp[k, at_z(2)] + zu[k]
+        remote(tp.at[k, at_z(2), other], zhu.at[k, 1], k, HALF_U, up_other).start()
+        remote(tp.at[k, at_z(2), ylo], zhu.at[k, 0], k, HALF_U, up).start()
+        sent.append(remote(zhu.at[k], zhu.at[k], k, HALF_U, up))
+        remote(zd.at[k], zd.at[k], k, RD + 1, down).wait_recv()
+        tp[k, at_z(-2)] = tp[k, at_z(-2)] + zd[k]
+        remote(tp.at[k, at_z(-2), other], zhd.at[k, 1], k, HALF_D, down_other).start()
+        remote(tp.at[k, at_z(-2), ylo], zhd.at[k, 0], k, HALF_D, down).start()
+        sent.append(remote(zhd.at[k], zhd.at[k], k, HALF_D, down))
 
     def z4(k):
-        remote(zu.at[k, 1], zu.at[k, 1], k, RU + 2, up).wait_recv()
-        tp[k, z_up] = tp[k, z_up] + zu[k, 1]
-        remote(tp.at[k, z_up, other], zl.at[k, 2], k, LAST, up_other).start()
+        remote(yo.at[k], yo.at[k], k, OWN, ypart).wait_recv()
+        remote(zhu.at[k], zhu.at[k], k, HALF_U, up).wait_recv()
+        tp[k, z_up, ylo] = tp[k, z_up, ylo] + (yo[k, 0] + (zhu[k, 0] + zhu[k, 1]))
         remote(tp.at[k, z_up, ylo], zl.at[k, 0], k, LAST, up).start()
-        remote(zd.at[k, 1], zd.at[k, 1], k, RD + 2, down).wait_recv()
-        tp[k, z_down] = tp[k, z_down] + zd[k, 1]
-        remote(tp.at[k, z_down, other], zl.at[k, 3], k, LAST, down_other).start()
+        remote(zhd.at[k], zhd.at[k], k, HALF_D, down).wait_recv()
+        tp[k, z_down, ylo] = tp[k, z_down, ylo] + (yo[k, 1] + (zhd[k, 0] + zhd[k, 1]))
         remote(tp.at[k, z_down, ylo], zl.at[k, 1], k, LAST, down).start()
         sent.append(remote(zl.at[k], zl.at[k], k, LAST, up))
 
     def z6(k):
         remote(zl.at[k], zl.at[k], k, LAST, up).wait_recv()
-        total = tp[k, z, ylo]
-        for d in range(5):
-            total = total + zl[k, d]
-        tf[k, z, ylo] = total
-        for device in (up_other, down_other, up, down, ypart):
+        tf[k, z, ylo] = tp[k, z, ylo] + (yo[k, 2] + (zl[k, 0] + zl[k, 1]))
+        for device in (up, down, ypart):
             remote(tf.at[k, z, ylo], tf.at[k, z, ylo], k, FIRST, device).start()
-        sent.append(remote(zl.at[k], zl.at[k], k, FIRST, up))
+        sent.append(remote(yo.at[k], yo.at[k], k, FIRST, up))
 
     def z7(k):
-        remote(zl.at[k], zl.at[k], k, FIRST, up).wait_recv()
-        push(tf.at[k, z_down], tf.at[k, z_down], k, GU, up)
-        push(tf.at[k, z_up], tf.at[k, z_up], k, GD, down)
+        remote(yo.at[k], yo.at[k], k, FIRST, up).wait_recv()
+        below, above = tf.at[k, z_down, ylo], tf.at[k, z_up, ylo]
+        remote(below, below, k, PASS_U, up_other).start()
+        remote(below, below, k, PASS_U, up).start()
+        remote(above, above, k, PASS_D, down_other).start()
+        remote(above, above, k, PASS_D, down).start()
+        remote(below, below, k, NEAR, ypart).start()
+        remote(above, above, k, NEAR, ypart).start()
+        for sem in (PASS_U, PASS_D, NEAR):
+            sent.append(remote(zl.at[k], zl.at[k], k, sem, up))
 
     def z8(k):
-        below, above = at_z(-2), at_z(2)
-        remote(tf.at[k, below], tf.at[k, below], k, GU, up).wait_recv()
-        push(tf.at[k, below], tf.at[k, below], k, GU + 1, up)
-        remote(tf.at[k, above], tf.at[k, above], k, GD, down).wait_recv()
-        push(tf.at[k, above], tf.at[k, above], k, GD + 1, down)
+        below, above = tf.at[k, at_z(-2)], tf.at[k, at_z(2)]
+        remote(zl.at[k], zl.at[k], k, PASS_U, up).wait_recv()
+        push(below, below, k, GU, up)
+        remote(zl.at[k], zl.at[k], k, PASS_D, down).wait_recv()
+        push(above, above, k, GD, down)
+
+    def p1(k):
+        remote(zl.at[k], zl.at[k], k, NEAR, ypart).wait_recv()
+        product_two(k, 0)
 
     def z9(k):
         below, above = at_z(-3), at_z(3)
-        remote(tf.at[k, below], tf.at[k, below], k, GU + 1, up).wait_recv()
-        push(tf.at[k, below, 0], tf.at[k, below, 0], k, GU + 2, up)
-        remote(tf.at[k, above], tf.at[k, above], k, GD + 1, down).wait_recv()
-        push(tf.at[k, above, 1], tf.at[k, above, 1], k, GD + 2, down)
+        remote(tf.at[k, below], tf.at[k, below], k, GU, up).wait_recv()
+        push(tf.at[k, below, 0], tf.at[k, below, 0], k, GU + 1, up)
+        remote(tf.at[k, above], tf.at[k, above], k, GD, down).wait_recv()
+        push(tf.at[k, above, 1], tf.at[k, above, 1], k, GD + 1, down)
 
     def z11(k):
         far = at_z(4)
-        remote(tf.at[k, far, 0], tf.at[k, far, 0], k, GU + 2, up).wait_recv()
-        remote(tf.at[k, far, 1], tf.at[k, far, 1], k, GD + 2, down).wait_recv()
+        remote(tf.at[k, far, 0], tf.at[k, far, 0], k, GU + 1, up).wait_recv()
+        remote(tf.at[k, far, 1], tf.at[k, far, 1], k, GD + 1, down).wait_recv()
         product_two(k, 3)
         push(ob.at[k, 1 - core], oc.at[k], k, CORE_O, sib)
 
@@ -264,7 +277,7 @@
 
     stages = {
         "A0": a0, "A1": a1, "A2": a2, "A3": a3, "A4": a4, "A4b": a4b, "Z2": z2, "Z3": z3, "Z4": z4, "Z6": z6,
-        "Z7": z7, "P1": lambda k: product_two(k, 0), "Z8": z8, "P2": lambda k: product_two(k, 1),
+        "Z7": z7, "P1": p1, "Z8": z8, "P2": lambda k: product_two(k, 1),
         "Z9": z9, "P3": lambda k: product_two(k, 2), "Z11": z11, "B1": b1, "B2": b2,
         "x_load": lambda k: x_load(), "h_prep": lambda k: h_prep(), "x_prep": lambda k: x_prep(),
     }
@@ -297,8 +310,9 @@
             pltpu.VMEM((CHUNKS, 2 * ROWS, n), bf16), pltpu.VMEM((2 * ROWS, 2 * EDGE), bf16),
             pltpu.VMEM((CHUNKS, RING, 2, *part), f32),
             pltpu.VMEM((CHUNKS, *part), f32), pltpu.VMEM((CHUNKS, *part), f32),
-            pltpu.VMEM((CHUNKS, 2, 2, *part), f32), pltpu.VMEM((CHUNKS, 2, 2, *part), f32),
-            pltpu.VMEM((CHUNKS, 5, *part), f32),
+            pltpu.VMEM((CHUNKS, 2, *part), f32), pltpu.VMEM((CHUNKS, 2, *part), f32),
+            pltpu.VMEM((CHUNKS, 2, *part), f32), pltpu.VMEM((CHUNKS, 2, *part), f32),
+            pltpu.VMEM((CHUNKS, 2, *part), f32), pltpu.VMEM((CHUNKS, 3, *part), f32),
             pltpu.VMEM((CHUNKS, RING, 2, *part), f32),
             pltpu.VMEM((CHUNKS, 2, CHIPS, slab, n), f32),
             pltpu.VMEM((CHUNKS, CHIPS, slab, n), f32),

time: 92.6 us -> 89.2 us (0.963)
  Pallas kernels: 90.2 us -> 86.8 us
    pallas_call x1, Pallas kernels: 90.2 us -> 86.8 us  [on_device(): pl.pallas_call(kernel, out_shape=jax.ShapeDtypeStruct((CHUNKS, slab, n),...]
where the time goes in v3:
time: 89.2 us; the launch traced here: 89.1 us
  Pallas kernels  86.8 us (97%)
  local copies, waits for them, and re-layouts  1.57 us (2%)
    pallas_call x1, Pallas kernels, on_device(): pl.pallas_call(kernel, out_shape=jax.ShapeDtypeStruct((CHUNKS, slab, n),...  86.8 us

profile of v3, /device:TPU:1, one launch (start us, length us, event | category | flops | bytes accessed | tf_op | source)
XLA Modules:
  0.0 89.1 jit_solution(15435333465977891204)
XLA Ops:
  0.7 86.8 %shard_map.55 = f32[4,8,1024]{2,1,0:T(8,128)} custom-call(f32[2,8,2,4,8,1024]{5,4,3,2,1,0:T(8,128)} %bitcast.2, f32[1024,1024]{1,0:T(8,128)} %h_hbm.1, s32[8,8]{1,0:T(8,128)} %xm_ref.1, s32[8,8]{1,0:T(8,128)} %hm_ref.1, s32[1]{0:T(128)S(6)} %copy.7.panel_ref), custom_call_target="tpu_custom_call" | custom-call | tf_op jit(solution)/shard_map/pallas_call | solution.py:295
  87.5 1.6 %copy.8 = f32[32,1024]{1,0:T(8,128)} copy(f32[32,1024]{1,0:T(8,128)} %bitcast.3) | data formatting | bytes 262144

commit v4 on v3

--- a/solution.py
+++ b/solution.py
@@ -16,15 +16,15 @@
 EDGE = 128
 
 ORDER = (
-    ("x_load", 0), ("A0", 2), ("A0", 3), ("A0", 1), ("A1", 2), ("A1", 3), ("A1", 1), ("A0", 0), ("A1", 0),
-    ("A2", 2), ("A2", 3), ("A2", 1), ("h_prep", 0), ("A2", 0), ("x_prep", 0), ("A3", 2), ("A4", 2), ("A4b", 2),
-    ("A3", 3), ("A4", 3), ("Z2", 2), ("A3", 1), ("A4b", 3), ("A4", 1), ("A4b", 1), ("A3", 0), ("Z2", 3),
-    ("Z3", 2), ("A4", 0), ("Z2", 1), ("A4b", 0), ("Z3", 3), ("Z4", 2), ("Z2", 0), ("Z3", 1), ("Z4", 3), ("Z6", 2),
-    ("Z3", 0), ("Z4", 1), ("Z6", 3), ("Z7", 2), ("Z4", 0), ("Z6", 1), ("Z7", 3), ("Z8", 2), ("P1", 2), ("Z6", 0),
-    ("Z7", 1), ("Z8", 3), ("P1", 3), ("Z9", 2), ("P2", 2), ("Z7", 0), ("P3", 2), ("Z8", 1), ("P1", 1), ("Z11", 2),
-    ("Z9", 3), ("P2", 3), ("P3", 3), ("B1", 2), ("Z8", 0), ("P1", 0), ("Z9", 1), ("P2", 1), ("P3", 1), ("Z11", 3),
-    ("B1", 3), ("Z9", 0), ("P2", 0), ("Z11", 1), ("B2", 2), ("B1", 1), ("P3", 0), ("Z11", 0), ("B1", 0),
-    ("B2", 3), ("B2", 0), ("B2", 1),
+    ("x_load", 0), ("A0", 3), ("A1", 3), ("A0", 0), ("A1", 0), ("A0", 2), ("A1", 2), ("A2", 3), ("h_prep", 0),
+    ("A2", 0), ("A0", 1), ("A1", 1), ("x_prep", 0), ("A3", 3), ("A4", 3), ("A2", 2), ("A3", 0), ("A4b", 3),
+    ("A4", 0), ("Z2", 3), ("A2", 1), ("A4b", 0), ("Z2", 0), ("A3", 2), ("A4", 2), ("Z3", 3), ("A3", 1), ("Z3", 0),
+    ("A4b", 2), ("A4", 1), ("Z2", 2), ("A4b", 1), ("Z4", 3), ("Z4", 0), ("Z2", 1), ("Z3", 2), ("Z6", 3),
+    ("Z6", 0), ("Z3", 1), ("Z4", 2), ("Z7", 3), ("Z4", 1), ("Z6", 2), ("Z7", 0), ("Z8", 3), ("Z6", 1), ("Z7", 2),
+    ("Z8", 0), ("P1", 3), ("Z9", 3), ("Z7", 1), ("Z8", 2), ("P1", 2), ("P1", 0), ("Z9", 0), ("P2", 3), ("P3", 3),
+    ("Z11", 3), ("P2", 0), ("P3", 0), ("Z8", 1), ("B1", 3), ("Z9", 2), ("P2", 2), ("P3", 2), ("Z11", 0),
+    ("B1", 0), ("P1", 1), ("Z9", 1), ("Z11", 2), ("B1", 2), ("P2", 1), ("P3", 1), ("Z11", 1), ("B1", 1),
+    ("B2", 2), ("B2", 3), ("B2", 0), ("B2", 1),
 )
 
 CORE_P, DIR_P, AG_P, CORE_R, CORE_O, DIR_O, OWN, HALF_U, HALF_D, LAST, FIRST, NEAR, PASS_U, PASS_D = range(14)
@@ -32,8 +32,8 @@
 N_SEMS = 22
 
 
-def kernel(x_hbm, h_hbm, xm_ref, hm_ref, panel_ref, out_ref,
-           xv, hv, xh, xl, hh, hl, wx, mx, mh, piece, pc, pr, rr, ab, tb, tp, zu1, zd1, zu, zd, zhu, zhd, zl, yo, tf,
+def kernel(x_hbm, h_hbm, xm_hbm, hm_hbm, panel_ref, out_ref,
+           xm_ref, hm_ref, xv, hv, xh, xl, hh, hl, wx, mx, mh, piece, pc, pr, rr, ab, tb, tp, zu1, zd1, zu, zd, zhu, zhd, zl, yo, tf,
            ob, oc, orv, load_sem, send, recv):
     row, col = lax.axis_index("row"), lax.axis_index("col")
     core, chip = lax.rem(row, 2), lax.div(row, 2)
@@ -54,7 +54,11 @@
 
     load_x = pltpu.make_async_copy(x_hbm, xv, load_sem.at[0])
     load_h = pltpu.make_async_copy(h_hbm, hv, load_sem.at[1])
+    load_xm = pltpu.make_async_copy(xm_hbm, xm_ref, load_sem.at[2])
+    load_hm = pltpu.make_async_copy(hm_hbm, hm_ref, load_sem.at[3])
+    load_xm.start()
     load_x.start()
+    load_hm.start()
 
     barrier = pltpu.get_barrier_semaphore()
     friends = [sib] + around + [peer(d) for d in range(1, CHIPS)]
@@ -109,6 +113,7 @@
             ob[k, :, :, :, n:n + 256] = value if step == 0 else ob[k, :, :, :, n:n + 256] + value
 
     def x_load():
+        load_xm.wait()
         mx[...] = spread(xm_ref[...])
         s0 = jnp.where(panel_ref[0] == 2 * row, 1.0, 0.0)
         s1 = jnp.where(panel_ref[0] == 2 * row + 1, 1.0, 0.0)
@@ -118,6 +123,7 @@
         load_h.start()
 
     def h_prep():
+        load_hm.wait()
         mh[...] = spread(hm_ref[...])
         load_h.wait()
 
@@ -294,10 +300,11 @@
     vmem, hbm = pl.BlockSpec(memory_space=pltpu.VMEM), pl.BlockSpec(memory_space=pl.ANY)
     out = pl.pallas_call(
         kernel,
-        out_shape=jax.ShapeDtypeStruct((CHUNKS, slab, n), f32),
-        in_specs=[hbm, hbm, vmem, vmem, pl.BlockSpec(memory_space=pltpu.SMEM)],
+        out_shape=pltpu.VMEM((CHUNKS, slab, n), f32),
+        in_specs=[hbm, hbm, hbm, hbm, pl.BlockSpec(memory_space=pltpu.SMEM)],
         out_specs=vmem,
         scratch_shapes=[
+            pltpu.VMEM((8, 8), jnp.int32), pltpu.VMEM((8, 8), jnp.int32),
             pltpu.VMEM((2, CHIPS, 2, CHUNKS, slab, n), f32),
             pltpu.VMEM((n, n), f32),
             pltpu.VMEM((n, n), bf16), pltpu.VMEM((n, n), bf16),
@@ -317,7 +324,7 @@
             pltpu.VMEM((CHUNKS, 2, CHIPS, slab, n), f32),
             pltpu.VMEM((CHUNKS, CHIPS, slab, n), f32),
             pltpu.VMEM((CHUNKS, CHIPS - 1, slab, n), f32),
-            pltpu.SemaphoreType.DMA((2,)),
+            pltpu.SemaphoreType.DMA((4,)),
             pltpu.SemaphoreType.DMA((CHUNKS, N_SEMS)),
             pltpu.SemaphoreType.DMA((CHUNKS, N_SEMS)),
         ],

time: 89.2 us -> 86.2 us (0.966)
  Pallas kernels: 86.8 us -> 84.8 us
  local copies, waits for them, and re-layouts: 1.57 us -> 0.66 us
    pallas_call x1, Pallas kernels: 86.8 us -> 84.8 us  [on_device(): pl.pallas_call(kernel, out_shape=pltpu.VMEM((CHUNKS, slab, n), f32), in_s...]
    unnamed x1, local copies, waits for them, and re-layouts: 1.57 us -> 0.66 us
where the time goes in v4:
time: 86.2 us; the launch traced here: 86.1 us
  Pallas kernels  84.8 us (98%)
    pallas_call x1, Pallas kernels, on_device(): pl.pallas_call(kernel, out_shape=pltpu.VMEM((CHUNKS, slab, n), f32), in_s...  84.8 us

profile of v4, /device:TPU:1, one launch (start us, length us, event | category | flops | bytes accessed | tf_op | source)
XLA Modules:
  0.0 86.1 jit_solution(15573984898504960315)
XLA Ops:
  0.7 84.8 %shard_map.55 = f32[4,8,1024]{2,1,0:T(8,128)S(1)} custom-call(f32[2,8,2,4,8,1024]{5,4,3,2,1,0:T(8,128)} %bitcast.3, f32[1024,1024]{1,0:T(8,128)} %h_hbm.1, s32[8,8]{1,0:T(8,128)} %xm_hbm.1, s32[8,8]{1,0:T(8,128)} %hm_hbm.1, s32[1]{0:T(128)S(6)} %copy.8.panel_ref), custom_call_target="tpu_custom_call" | custom-call | tf_op jit(solution)/shard_map/pallas_call | solution.py:301
  85.4 0.7 copy.7

commit v5 on v4

--- a/solution.py
+++ b/solution.py
@@ -15,16 +15,18 @@
 RING = 8
 EDGE = 128
 
+SHORT_SUM = (0, 1, 2, 3)
+SHORT_GATHER = (0, 1, 2, 3)
+
 ORDER = (
-    ("x_load", 0), ("A0", 3), ("A1", 3), ("A0", 0), ("A1", 0), ("A0", 2), ("A1", 2), ("A2", 3), ("h_prep", 0),
-    ("A2", 0), ("A0", 1), ("A1", 1), ("x_prep", 0), ("A3", 3), ("A4", 3), ("A2", 2), ("A3", 0), ("A4b", 3),
-    ("A4", 0), ("Z2", 3), ("A2", 1), ("A4b", 0), ("Z2", 0), ("A3", 2), ("A4", 2), ("Z3", 3), ("A3", 1), ("Z3", 0),
-    ("A4b", 2), ("A4", 1), ("Z2", 2), ("A4b", 1), ("Z4", 3), ("Z4", 0), ("Z2", 1), ("Z3", 2), ("Z6", 3),
-    ("Z6", 0), ("Z3", 1), ("Z4", 2), ("Z7", 3), ("Z4", 1), ("Z6", 2), ("Z7", 0), ("Z8", 3), ("Z6", 1), ("Z7", 2),
-    ("Z8", 0), ("P1", 3), ("Z9", 3), ("Z7", 1), ("Z8", 2), ("P1", 2), ("P1", 0), ("Z9", 0), ("P2", 3), ("P3", 3),
-    ("Z11", 3), ("P2", 0), ("P3", 0), ("Z8", 1), ("B1", 3), ("Z9", 2), ("P2", 2), ("P3", 2), ("Z11", 0),
-    ("B1", 0), ("P1", 1), ("Z9", 1), ("Z11", 2), ("B1", 2), ("P2", 1), ("P3", 1), ("Z11", 1), ("B1", 1),
-    ("B2", 2), ("B2", 3), ("B2", 0), ("B2", 1),
+    ("x_load", 0), ("A0", 0), ("A1", 0), ("A0", 2), ("A1", 2), ("A0", 1), ("A0", 3), ("A1", 1), ("A2", 0),
+    ("h_prep", 0), ("A2", 2), ("A1", 3), ("A3", 0), ("A2", 1), ("A4", 0), ("A4b", 0), ("A3", 2), ("A4", 2),
+    ("A2", 3), ("A3", 1), ("Z3", 0), ("A4", 1), ("A4b", 2), ("Z3", 2), ("A4b", 1), ("A3", 3), ("Z4", 0),
+    ("A4", 3), ("A4b", 3), ("Z3", 1), ("Z4", 2), ("Z6", 0), ("x_prep", 0), ("Z3", 3), ("Z4", 1), ("Z6", 2),
+    ("Z7", 0), ("Z4", 3), ("Z6", 1), ("Z7", 2), ("Z8", 0), ("Z6", 3), ("Z7", 1), ("Z8", 2), ("P1", 0), ("Z7", 3),
+    ("P1", 2), ("P2", 0), ("Z11", 0), ("Z8", 1), ("P1", 1), ("P2", 2), ("B1", 0), ("Z11", 2), ("Z8", 3),
+    ("P1", 3), ("P2", 3), ("B1", 2), ("P2", 1), ("Z11", 1), ("B1", 1), ("B2", 0), ("Z11", 3), ("B1", 3),
+    ("B2", 1), ("B2", 2), ("B2", 3),
 )
 
 CORE_P, DIR_P, AG_P, CORE_R, CORE_O, DIR_O, OWN, HALF_U, HALF_D, LAST, FIRST, NEAR, PASS_U, PASS_D = range(14)
@@ -39,18 +41,19 @@
     core, chip = lax.rem(row, 2), lax.div(row, 2)
     z, ylo = lax.rem(col, RING), lax.div(col, RING)
     sib = (row + 1 - 2 * core, col)
+    def at_z(d):
+        return lax.rem(z + (d + RING) % RING, RING)
+
     other = 1 - ylo
     ypart = (row, other * RING + z)
     z_up, z_down = lax.rem(z + 1, RING), lax.rem(z + RING - 1, RING)
     up, up_other = (row, ylo * RING + z_up), (row, other * RING + z_up)
     down, down_other = (row, ylo * RING + z_down), (row, other * RING + z_down)
-    around = [up, down, up_other, down_other, ypart]
+    up_two, down_two = (row, ylo * RING + at_z(2)), (row, ylo * RING + at_z(-2))
+    around = [up_two, down_two, up, down, up_other, down_other, ypart]
 
     def peer(d):
         return (lax.rem(chip + d, CHIPS) * 2 + core, col)
-
-    def at_z(d):
-        return lax.rem(z + (d + RING) % RING, RING)
 
     load_x = pltpu.make_async_copy(x_hbm, xv, load_sem.at[0])
     load_h = pltpu.make_async_copy(h_hbm, hv, load_sem.at[1])
@@ -183,11 +186,18 @@
         ab[k, 0:ROWS, :] = high
         ab[k, ROWS:, :] = low
         product_one(k, 0)
-        push(tp.at[k, at_z(4), 0], zu1.at[k], k, RU, up)
-        push(tp.at[k, at_z(4), 1], zd1.at[k], k, RD, down)
+        if k in SHORT_SUM:
+            product_one(k, 1)
+            push(tp.at[k, at_z(4), 0], zu1.at[k], k, RU, up_two)
+            push(tp.at[k, at_z(4), 1], zd1.at[k], k, RD, down_two)
+            push(tp.at[k, at_z(3)], zu.at[k], k, RU + 1, up)
+            push(tp.at[k, at_z(-3)], zd.at[k], k, RD + 1, down)
+        else:
+            push(tp.at[k, at_z(4), 0], zu1.at[k], k, RU, up)
+            push(tp.at[k, at_z(4), 1], zd1.at[k], k, RD, down)
 
     def a4b(k):
-        for step in (1, 2, 3):
+        for step in (2, 3) if k in SHORT_SUM else (1, 2, 3):
             product_one(k, step)
         for slot, owner in enumerate((z_up, z_down, z)):
             remote(tp.at[k, owner, other], yo.at[k, slot], k, OWN, ypart).start()
@@ -202,6 +212,11 @@
         push(tp.at[k, at_z(-3)], zd.at[k], k, RD + 1, down)
 
     def z3(k):
+        if k in SHORT_SUM:
+            remote(zu1.at[k], zu1.at[k], k, RU, up).wait_recv()
+            tp[k, at_z(2), 0] = tp[k, at_z(2), 0] + zu1[k]
+            remote(zd1.at[k], zd1.at[k], k, RD, down).wait_recv()
+            tp[k, at_z(-2), 1] = tp[k, at_z(-2), 1] + zd1[k]
         remote(zu.at[k], zu.at[k], k, RU + 1, up).wait_recv()
         tp[k, at_z(2)] = tp[k, at_z(2)] + zu[k]
         remote(tp.at[k, at_z(2), other], zhu.at[k, 1], k, HALF_U, up_other).start()
@@ -245,8 +260,12 @@
     def z8(k):
         below, above = tf.at[k, at_z(-2)], tf.at[k, at_z(2)]
         remote(zl.at[k], zl.at[k], k, PASS_U, up).wait_recv()
+        if k in SHORT_GATHER:
+            push(below.at[0], below.at[0], k, GU + 1, up_two)
         push(below, below, k, GU, up)
         remote(zl.at[k], zl.at[k], k, PASS_D, down).wait_recv()
+        if k in SHORT_GATHER:
+            push(above.at[1], above.at[1], k, GD + 1, down_two)
         push(above, above, k, GD, down)
 
     def p1(k):
@@ -264,6 +283,11 @@
         far = at_z(4)
         remote(tf.at[k, far, 0], tf.at[k, far, 0], k, GU + 1, up).wait_recv()
         remote(tf.at[k, far, 1], tf.at[k, far, 1], k, GD + 1, down).wait_recv()
+        if k in SHORT_GATHER:
+            below, above = at_z(-3), at_z(3)
+            remote(tf.at[k, below], tf.at[k, below], k, GU, up).wait_recv()
+            remote(tf.at[k, above], tf.at[k, above], k, GD, down).wait_recv()
+            product_two(k, 2)
         product_two(k, 3)
         push(ob.at[k, 1 - core], oc.at[k], k, CORE_O, sib)
 

time: 86.2 us -> 84.2 us (0.977)
  Pallas kernels: 84.8 us -> 82.7 us
    pallas_call x1, Pallas kernels: 84.8 us -> 82.7 us  [on_device(): pl.pallas_call(kernel, out_shape=pltpu.VMEM((CHUNKS, slab, n), f32), in_s...]
where the time goes in v5:
time: 84.2 us; the launch traced here: 84.1 us
  Pallas kernels  82.7 us (98%)
    pallas_call x1, Pallas kernels, on_device(): pl.pallas_call(kernel, out_shape=pltpu.VMEM((CHUNKS, slab, n), f32), in_s...  82.7 us

profile of v5, /device:TPU:1, one launch (start us, length us, event | category | flops | bytes accessed | tf_op | source)
XLA Modules:
  0.0 84.1 jit_solution(7453475247631037993)
XLA Ops:
  0.7 82.7 %shard_map.55 = f32[4,8,1024]{2,1,0:T(8,128)S(1)} custom-call(f32[2,8,2,4,8,1024]{5,4,3,2,1,0:T(8,128)} %bitcast.3, f32[1024,1024]{1,0:T(8,128)} %h_hbm.1, s32[8,8]{1,0:T(8,128)} %xm_hbm.1, s32[8,8]{1,0:T(8,128)} %hm_hbm.1, s32[1]{0:T(128)S(6)} %copy.8.panel_ref), custom_call_target="tpu_custom_call" | custom-call | tf_op jit(solution)/shard_map/pallas_call | solution.py:325
  83.4 0.7 copy.7

commit v6 on v5

--- a/solution.py
+++ b/solution.py
@@ -14,6 +14,7 @@
 CHIPS = 8
 RING = 8
 EDGE = 128
+FAR_FIRST = (5, 3, 4, 7, 1, 2, 6)
 
 SHORT_SUM = (0, 1, 2, 3)
 SHORT_GATHER = (0, 1, 2, 3)
@@ -94,9 +95,8 @@
         turn = 1 - 2 * lax.rem(z + 1, 2)
         pair = lax.rem(far + (0, 4 + turn, 4 - turn, 2)[step], 4)
         rows = pl.ds(pl.multiple_of(pair * 256, 256), 256)
-        dims = (((1,), (1,)), ((), ()))
-        first = lax.dot_general(ab[k], hh[rows, :], dims, preferred_element_type=jnp.float32)
-        second = lax.dot_general(ab[k, 0:ROWS, :], hl[rows, :], dims, preferred_element_type=jnp.float32)
+        first = jnp.dot(ab[k], hh[:, rows], preferred_element_type=jnp.float32)
+        second = jnp.dot(ab[k, 0:ROWS, :], hl[:, rows], preferred_element_type=jnp.float32)
         value = first[:ROWS] + (first[ROWS:] + second)
         tp[k, 2 * pair] = value[:, :EDGE].reshape(2, ROWS // 2, EDGE)
         tp[k, 2 * pair + 1] = value[:, EDGE:].reshape(2, ROWS // 2, EDGE)
@@ -132,9 +132,9 @@
 
         def body(b, carry):
             rows = pl.ds(pl.multiple_of(b * EDGE, EDGE), EDGE)
-            high, low = split(hv[rows, :] * mh[pl.ds(b, 1), :])
-            hh[rows, :] = high
-            hl[rows, :] = low
+            high, low = split((hv[rows, :] * mh[pl.ds(b, 1), :]).T)
+            hh[:, rows] = high
+            hl[:, rows] = low
             return carry
 
         lax.fori_loop(0, 8, body, 0)
@@ -162,7 +162,7 @@
     def a1(k):
         remote(pc.at[k], pc.at[k], k, CORE_P, sib).wait_recv()
         piece[k, core] = piece[k, core] + pc[k]
-        for d in range(1, CHIPS):
+        for d in FAR_FIRST:
             remote(piece.at[k, core, lax.rem(chip + d, CHIPS)], pr.at[k, d - 1], k, DIR_P, peer(d)).start()
         sent.append(remote(pr.at[k], pr.at[k], k, DIR_P, sib))
 
@@ -172,7 +172,7 @@
         for d in range(CHIPS - 1):
             total = total + pr[k, d]
         rr[k, core, chip] = total
-        for d in range(1, CHIPS):
+        for d in FAR_FIRST:
             remote(rr.at[k, core, chip], rr.at[k, core, chip], k, AG_P, peer(d)).start()
         sent.append(remote(pr.at[k], pr.at[k], k, AG_P, sib))
 
@@ -294,7 +294,7 @@
     def b1(k):
         remote(oc.at[k], oc.at[k], k, CORE_O, sib).wait_recv()
         ob[k, core] = ob[k, core] + oc[k]
-        for d in range(1, CHIPS):
+        for d in FAR_FIRST:
             remote(ob.at[k, core, lax.rem(chip + d, CHIPS)], orv.at[k, d - 1], k, DIR_O, peer(d)).start()
         sent.append(remote(orv.at[k], orv.at[k], k, DIR_O, sib))
 
@@ -311,8 +311,13 @@
         "Z9": z9, "P3": lambda k: product_two(k, 2), "Z11": z11, "B1": b1, "B2": b2,
         "x_load": lambda k: x_load(), "h_prep": lambda k: h_prep(), "x_prep": lambda k: x_prep(),
     }
-    for name, k in ORDER:
+    last = max(i for i, (name, _) in enumerate(ORDER) if name == "B1")
+    for i, (name, k) in enumerate(ORDER):
         stages[name](k)
+        if i == last:
+            for copy in sent[:-1]:
+                copy.wait_send()
+            del sent[:-1]
     for copy in sent:
         copy.wait_send()
 

time: 84.2 us -> 83.8 us (level)
  no operation moved by 1% of the time
where the time goes in v6:
time: 83.8 us; the launch traced here: 83.7 us
  Pallas kernels  82.4 us (98%)
    pallas_call x1, Pallas kernels, on_device(): pl.pallas_call(kernel, out_shape=pltpu.VMEM((CHUNKS, slab, n), f32), in_s...  82.4 us

profile of v6, /device:TPU:1, one launch (start us, length us, event | category | flops | bytes accessed | tf_op | source)
XLA Modules:
  0.0 83.7 jit_solution(15843782320159354315)
XLA Ops:
  0.7 82.4 %shard_map.55 = f32[4,8,1024]{2,1,0:T(8,128)S(1)} custom-call(f32[2,8,2,4,8,1024]{5,4,3,2,1,0:T(8,128)} %bitcast.3, f32[1024,1024]{1,0:T(8,128)} %h_hbm.1, s32[8,8]{1,0:T(8,128)} %xm_hbm.1, s32[8,8]{1,0:T(8,128)} %hm_hbm.1, s32[1]{0:T(128)S(6)} %copy.8.panel_ref), custom_call_target="tpu_custom_call" | custom-call | tf_op jit(solution)/shard_map/pallas_call | solution.py:330
  83.0 0.7 copy.7

commit v7 on v6

--- a/solution.py
+++ b/solution.py
@@ -101,7 +101,7 @@
         tp[k, 2 * pair] = value[:, :EDGE].reshape(2, ROWS // 2, EDGE)
         tp[k, 2 * pair + 1] = value[:, EDGE:].reshape(2, ROWS // 2, EDGE)
 
-    def product_two(k, step):
+    def product_two(k, step, ready=None):
         turn = 1 - 2 * lax.rem(z + 1, 2)
         pair = lax.rem(lax.div(z, 2) + (0, 4 + turn, 4 - turn, 2)[step], 4)
         for half in range(2):
@@ -114,6 +114,8 @@
             second = jnp.dot(tb[0:ROWS, :], xl[rows, n:n + 256], preferred_element_type=jnp.float32)
             value = (first[:ROWS] + (first[ROWS:] + second)).reshape(2, CHIPS, ROWS // 16, 256)
             ob[k, :, :, :, n:n + 256] = value if step == 0 else ob[k, :, :, :, n:n + 256] + value
+            if ready is not None and n % 512 == 256:
+                ready(n - 256)
 
     def x_load():
         load_xm.wait()
@@ -288,8 +290,12 @@
             remote(tf.at[k, below], tf.at[k, below], k, GU, up).wait_recv()
             remote(tf.at[k, above], tf.at[k, above], k, GD, down).wait_recv()
             product_two(k, 2)
-        product_two(k, 3)
-        push(ob.at[k, 1 - core], oc.at[k], k, CORE_O, sib)
+
+        def half(n):
+            remote(ob.at[k, 1 - core, :, :, n:n + 512], oc.at[k, :, :, n:n + 512], k, CORE_O, sib).start()
+
+        product_two(k, 3, half)
+        sent.append(remote(oc.at[k], oc.at[k], k, CORE_O, sib))
 
     def b1(k):
         remote(oc.at[k], oc.at[k], k, CORE_O, sib).wait_recv()

time: 83.8 us -> 84 us (level)
  no operation moved by 1% of the time
where the time goes in v7:
time: 84 us; the launch traced here: 83.9 us
  Pallas kernels  82.6 us (98%)
    pallas_call x1, Pallas kernels, on_device(): pl.pallas_call(kernel, out_shape=pltpu.VMEM((CHUNKS, slab, n), f32), in_s...  82.6 us

profile of v7, /device:TPU:1, one launch (start us, length us, event | category | flops | bytes accessed | tf_op | source)
XLA Modules:
  0.0 83.9 jit_solution(7682009895198708988)
XLA Ops:
  0.7 82.6 %shard_map.55 = f32[4,8,1024]{2,1,0:T(8,128)S(1)} custom-call(f32[2,8,2,4,8,1024]{5,4,3,2,1,0:T(8,128)} %bitcast.3, f32[1024,1024]{1,0:T(8,128)} %h_hbm.1, s32[8,8]{1,0:T(8,128)} %xm_hbm.1, s32[8,8]{1,0:T(8,128)} %hm_hbm.1, s32[1]{0:T(128)S(6)} %copy.8.panel_ref), custom_call_target="tpu_custom_call" | custom-call | tf_op jit(solution)/shard_map/pallas_call | solution.py:336
  83.2 0.7 copy.7
